TPU v7x, 32 devices: a whole 2x2x4 slice. The times are simulated.
32 devices in a mesh: dp: 8 (over z, y), mp: 4 (over x, core).
Axes of the slice: x: 2, y: 2, z: 4, core: 2. Of those that a mesh axis runs over, the one named last changes fastest.
Arguments:
- tokens: bfloat16 [8, 2048, 768], P('dp'), may hold values from -6 to 6
- cotangent: bfloat16 [8, 2048, 768], P('dp'), may hold values from -6 to 6
- capacity: int32 [8], replicated, may hold values from 256 to 1024, as said below
- selected: int32 [8, 1024], P('dp'), may hold values from 0 to 2047, as said below
- qkv_master: float32 [3, 768, 768], P(None, 'dp', 'mp'), may hold values from -0.21875 to 0.21875
- out_master: float32 [768, 768], P('mp', 'dp'), may hold values from -0.75 to 0.75
- up_master: float32 [768, 3072], P('dp', 'mp'), may hold values from -0.21875 to 0.21875
- down_master: float32 [3072, 768], P('mp', 'dp'), may hold values from -0.109375 to 0.109375
- vec_master: float32 [3, 768], P(None, 'dp')
- qkv_first: float32 [3, 768, 768], P(None, 'dp', 'mp'), may hold values from -48 to 48
- out_first: float32 [768, 768], P('mp', 'dp'), may hold values from -6 to 6
- up_first: float32 [768, 3072], P('dp', 'mp'), may hold values from -6 to 6
- down_first: float32 [3072, 768], P('mp', 'dp'), may hold values from -16 to 16
- vec_first: float32 [3, 768], P(None, 'dp')
- qkv_second: float32 [3, 768, 768], P(None, 'dp', 'mp'), may hold values from 127.7952 to 2064.384
- out_second: float32 [768, 768], P('mp', 'dp'), may hold values from 5.111808 to 82.57536
- up_second: float32 [768, 3072], P('dp', 'mp'), may hold values from 1.8402508 to 29.727129
- down_second: float32 [3072, 768], P('mp', 'dp'), may hold values from 14.057472 to 227.08224
- vec_second: float32 [3, 768], P(None, 'dp')
Outputs:
- block_out: bfloat16 [8, 2048, 768], P('dp')
- input_grad: float32 [8, 2048, 768], P('dp')
- qkv_new: float32 [3, 768, 768], P(None, 'dp', 'mp')
- out_new: float32 [768, 768], P('mp', 'dp')
- up_new: float32 [768, 3072], P('dp', 'mp')
- down_new: float32 [3072, 768], P('mp', 'dp')
- vec_new: float32 [3, 768], P(None, 'dp')
- qkv_first_new: float32 [3, 768, 768], P(None, 'dp', 'mp')
- out_first_new: float32 [768, 768], P('mp', 'dp')
- up_first_new: float32 [768, 3072], P('dp', 'mp')
- down_first_new: float32 [3072, 768], P('mp', 'dp')
- vec_first_new: float32 [3, 768], P(None, 'dp')
- qkv_second_new: float32 [3, 768, 768], P(None, 'dp', 'mp')
- out_second_new: float32 [768, 768], P('mp', 'dp')
- up_second_new: float32 [768, 3072], P('dp', 'mp')
- down_second_new: float32 [3072, 768], P('mp', 'dp')
- vec_second_new: float32 [3, 768], P(None, 'dp')
Inputs may be any that keep to these rules, and one draw needn't show every extreme that they name: Every sequence's capacity is 1024, 512 or 256; the sequences come in 4 batches of consecutive sequences that share one capacity, and each of the three values is used by some batch. Each row holds distinct positions: its first capacity[s] entries are the selected positions in ascending order, the rest are other positions in ascending order.
All inputs are finite; a program needn't handle non-finite values.
Results may differ from a plain program's by a relative error of at most 0.012.
Values may be sent and summed in bfloat16 or wider, within the bound.
A program may use at most 128 MiB of HBM per device.

v0:
```python
import functools

import jax
import jax.numpy as jnp
from jax import lax
from jax.experimental import pallas as pl
from jax.experimental.pallas import tpu as pltpu
from jax.sharding import PartitionSpec as P

HEAD_DIM = 64
STEP = 10
NORM_EPS = 1e-05
MASKED_SCORE = -1000000000.0
MOMENT_DECAY = 0.9
SQUARE_DECAY = 0.95
ADAM_EPS = 1e-08
WEIGHT_DECAY = 0.1
RATE_MATRIX = 0.06
RATE_VECTOR = 0.2

LOW = jnp.bfloat16
FULL = jnp.float32
MESH = pl.DeviceIdType.MESH
BLOCKS = 4
AROUND = (3,)
SPOT_ROWS = 512
VMEM_BYTES = 60 * 2**20


def nn(a, b):
    return lax.dot_general(a, b, (((1,), (0,)), ((), ())), preferred_element_type=FULL)


def nt(a, b):
    return lax.dot_general(a, b, (((1,), (1,)), ((), ())), preferred_element_type=FULL)


def tn(a, b):
    return lax.dot_general(a, b, (((0,), (0,)), ((), ())), preferred_element_type=FULL)


def mean_square_inverse(values):
    return lax.rsqrt(jnp.mean(values * values, axis=-1, keepdims=True) + NORM_EPS)


def gate_of(rows, router_row):
    width = rows.shape[-1]
    logit = jnp.sum(rows * router_row, axis=-1, keepdims=True) * width ** (-0.5)
    return jax.nn.sigmoid(logit)


def greet(partners):
    barrier = pltpu.get_barrier_semaphore()
    for partner in partners:
        pl.semaphore_signal(barrier, inc=1, device_id=partner, device_id_type=MESH)


def met(partners):
    pl.semaphore_wait(pltpu.get_barrier_semaphore(), len(partners))


def remote(src, dst, send_sem, recv_sem, device):
    return pltpu.make_async_remote_copy(
        src_ref=src,
        dst_ref=dst,
        send_sem=send_sem,
        recv_sem=recv_sem,
        device_id=device,
        device_id_type=MESH,
    )


class Exchange:
    def __init__(self, parts, near, pair, far, total, sems):
        self.parts, self.near, self.pair, self.far, self.total = parts, near, pair, far, total
        self.sems = sems
        self.me, self.part = lax.axis_index("dp"), lax.axis_index("mp")
        self.half = self.part % 2
        self.near_device = (self.me, self.part + 1 - 2 * self.half)
        self.far_device = (self.me, (self.part + 2) % 4)

    def copy(self, which, block, src, dst):
        device = self.far_device if which == 1 else self.near_device
        return remote(src, dst, self.sems.at[0, which, block], self.sems.at[1, which, block], device)

    def out(self, which, block):
        if which == 0:
            return self.copy(0, block, self.parts.at[block, 1 - self.half], self.near.at[block])
        if which == 1:
            return self.copy(1, block, self.pair.at[block], self.far.at[block])
        spot = self.total.at[block, self.half]
        return self.copy(2, block, spot, spot)

    def into(self, which, block):
        spot = (self.near.at[block], self.far.at[block], self.total.at[block, 1 - self.half])[which]
        return self.copy(which, block, spot, spot)

    def put(self, block, value):
        rows, width = value.shape
        self.parts[block] = value.astype(LOW).reshape(2, rows // 2, width)
        self.send(block)

    def send(self, block):
        self.out(0, block).start()

    def cross(self, block):
        self.into(0, block).wait_recv()
        self.pair[block] = (
            self.parts[block, self.half].astype(FULL) + self.near[block].astype(FULL)
        ).astype(LOW)
        self.out(1, block).start()

    def finish(self, block):
        self.into(1, block).wait_recv()
        self.total[block, self.half] = (
            self.pair[block].astype(FULL) + self.far[block].astype(FULL)
        ).astype(LOW)
        self.out(2, block).start()

    def arrived(self, block):
        self.into(2, block).wait_recv()

    def drain(self, block):
        for which in range(3):
            self.out(which, block).wait_send()


def head_lanes(width, head):
    lanes = lax.broadcasted_iota(jnp.int32, (1, width), 1)
    return (lanes // HEAD_DIM == head).astype(FULL).astype(LOW)


def main_kernel(groups, joined, *refs):
    (cap_ref, sel_ref, tok_any, cot_any), refs = refs[:4], refs[4:]
    if joined:
        masters, refs = refs[:5], refs[5:]
    else:
        (wg, gains), refs = refs[:2], refs[2:]
    (m_total, d_total, gsum_ref, vsum_ref), refs = refs[:4], refs[4:]
    (table, table_sems, x_ref, dy_ref, qkv_ref, o_ref, w4), refs = refs[:7], refs[7:]
    (parts, near, pair, far, a_total, a_sems, d_sems), refs = refs[:7], refs[7:]
    (h_parts, h_near, h_pair, h_far, h_total, h_sems), refs = refs[:6], refs[6:]
    (m_parts, m_near, m_pair, m_far, m_sems), refs = refs[:5], refs[5:]
    (slope_ref, dz_ref, out_acc, dkv, dlow, vacc, spot_ref, do_ref), refs = refs[:8], refs[8:]

    slots, width = x_ref.shape
    seq_len = tok_any.shape[0]
    local_width = o_ref.shape[1]
    heads = local_width // HEAD_DIM
    size = slots // BLOCKS
    me, part = lax.axis_index("dp"), lax.axis_index("mp")
    count = cap_ref[me]
    top = BLOCKS - 1

    def span(start):
        return pl.ds(pl.multiple_of(start, size), size)

    def rows_at(number):
        return span(number * size)

    def table_copy(which, source):
        return pltpu.make_async_copy(source, table.at[which], table_sems.at[which])

    table_copy(0, tok_any).start()
    table_copy(1, cot_any).start()

    heads_sum = Exchange(parts, near, pair, far, a_total, a_sems)
    hidden_sum = Exchange(h_parts, h_near, h_pair, h_far, h_total, h_sems)
    branch_sum = Exchange(m_parts, m_near, m_pair, m_far, m_total, m_sems)
    input_sum = Exchange(parts, near, pair, far, d_total, d_sems)
    partners = [heads_sum.near_device, heads_sum.far_device]

    if joined:
        (wg, gains, vg, send_r, recv_r, send_l, recv_l, send_f, recv_f), refs = refs[:9], refs[9:]
        (send_e, recv_e), refs = refs[:2], refs[2:]
        (grads, ry, pairs, rz, vpad, vr), refs = refs[:6], refs[6:]
        send_y, recv_y, send_z, recv_z, send_v, recv_v = refs
        line, place, side = groups // 2, me // 2, me % 2
        other = (me + 1 - 2 * side, part)
        everyone = [(lax.rem(me + j, groups), part) for j in range(1, groups)]

        half_share = width // groups // 2

        def slot(k, d):
            if k < 2:
                return wg.at[0, d, pl.ds(k * half_share, half_share)]
            return vg.at[d] if k == 4 else wg.at[k - 1, d]

        def chain(k, step, right):
            z = place - step + 1 if right else place + step - 1
            sems = (send_r, recv_r) if right else (send_l, recv_l)
            target = (me + 2 if right else me - 2, part)
            return remote(
                slot(k, z * 2 + side),
                slot(k, z * 2 + side),
                sems[0].at[k, step - 1],
                sems[1].at[k, step - 1],
                target,
            )

        def chain_in(k, step, right):
            z = place - step if right else place + step
            sems = (send_r, recv_r) if right else (send_l, recv_l)
            spot = slot(k, z * 2 + side)
            return remote(spot, spot, sems[0].at[k, step - 1], sems[1].at[k, step - 1], other)

        def can_send(step, right):
            if right:
                return (place + 1 < line) & (place - step + 1 >= 0)
            return (place >= 1) & (place + step - 1 < line)

        def across(k, z):
            spot = slot(k, z * 2 + side)
            return remote(spot, spot, send_f.at[k, z], recv_f.at[k, z], other)

        def across_in(k, z):
            spot = slot(k, z * 2 + 1 - side)
            return remote(spot, spot, send_f.at[k, z], recv_f.at[k, z], other)

        def begin_line(k):
            for right in (True, False):

                @pl.when(can_send(1, right))
                def _():
                    chain(k, 1, right).start()

        def begin_across(k):
            across(k, place).start()

        def round_about(k, z):
            if k not in AROUND:
                return False
            return ((place == 0) & (z == 1)) | ((place == line - 1) & (z == line - 2))

        def around(k, right):
            spot = slot(k, me + 1 - 2 * side)
            target = (me + 2 if right else me - 2, part)
            return remote(spot, spot, send_e.at[k], recv_e.at[k], target)

        def around_in(k, right):
            spot = slot(k, (me - 2 if right else me + 2) + 1 - 2 * side)
            return remote(spot, spot, send_e.at[k], recv_e.at[k], other)

        def turn(k):
            across_in(k, place).wait_recv()

            @pl.when(place == 1)
            def _():
                around(k, False).start()

            @pl.when(place == line - 2)
            def _():
                around(k, True).start()

        def pump(k, step):
            for right in (True, False):
                z = place - step if right else place + step

                @pl.when((z >= 0) & (z < line))
                def _():
                    chain_in(k, step, right).wait_recv()

                    if k in AROUND:

                        @pl.when(jnp.logical_not(round_about(k, z)))
                        def _():
                            across(k, z).start()

                    else:
                        across(k, z).start()

                if step + 1 < line:

                    @pl.when(can_send(step + 1, right))
                    def _():
                        chain(k, step + 1, right).start()

        def arrive(k):
            for z in range(line):
                if k in AROUND:

                    @pl.when(jnp.logical_not(round_about(k, z)) & (place != z))
                    def _():
                        across_in(k, z).wait_recv()

                else:
                    across_in(k, z).wait_recv()
            if k in AROUND:

                @pl.when(place == 0)
                def _():
                    around_in(k, False).wait_recv()

                @pl.when(place == line - 1)
                def _():
                    around_in(k, True).wait_recv()

        def drain_weights(k):
            for right in (True, False):
                for step in range(1, line):

                    @pl.when(can_send(step, right))
                    def _():
                        chain(k, step, right).wait_send()

            for z in range(line):
                if k in AROUND:

                    @pl.when(jnp.logical_not(round_about(k, z)))
                    def _():
                        across(k, z).wait_send()

                else:
                    across(k, z).wait_send()
            if k in AROUND:

                @pl.when(place == 1)
                def _():
                    around(k, False).wait_send()

                @pl.when(place == line - 2)
                def _():
                    around(k, True).wait_send()

        def plane(j):
            return lax.rem(place + j, line)

        def to_pair(k, j):
            spot = plane(j) * 2 + 1 - side
            return remote(
                grads.at[k, spot], ry.at[k, j - 1], send_y.at[k, j - 1], recv_y.at[k, j - 1], other
            )

        def to_line(k, j):
            return remote(
                pairs.at[k, j - 1],
                rz.at[k, j - 1],
                send_z.at[k, j - 1],
                recv_z.at[k, j - 1],
                (plane(j) * 2 + side, part),
            )

        def keep(k, value):
            grads[k] = value.astype(LOW).reshape(groups, width // groups, width)

        def give(k):
            for j in range(1, line + 1):
                to_pair(k, j).start()

        def relay(k, *which):
            for j in which:
                to_pair(k, j).wait_recv()
                own = grads[k, plane(j) * 2 + side].astype(FULL)
                pairs[k, j - 1] = (own + ry[k, j - 1].astype(FULL)).astype(LOW)
                if j < line:
                    to_line(k, j).start()

        def collect(k):
            total = pairs[k, line - 1].astype(FULL)
            for j in range(1, line):
                to_line(k, j).wait_recv()
                total = total + rz[k, j - 1].astype(FULL)
            gsum_ref[k] = total

        def to_all(j):
            target = lax.rem(me + j, groups)
            return remote(
                vpad.at[target], vr.at[j - 1], send_v.at[j - 1], recv_v.at[j - 1], (target, part)
            )

        greet(partners + everyone)
        qkv_m, out_m, up_m, down_m, vec_m = masters
        share = width // groups
        vg[me] = jnp.zeros((8, 128), FULL)
        vg[me, 0:3, :share] = vec_m[...].astype(LOW).astype(FULL)
        columns = [qkv_m[t] for t in range(3)] + [out_m[...].T]
        wg[0, me] = jnp.concatenate(columns, axis=1).astype(LOW)
        met(partners + everyone)
        for k in (0, 4, 1):
            begin_line(k)
            begin_across(k)
        wg[1, me] = up_m[...].astype(LOW)
        wg[2, me] = down_m[...].astype(LOW)
    else:
        greet(partners)
        met(partners)

        def keep(k, value):
            gsum_ref[k] = value

        def give(k):
            pass

        def relay(k, *which):
            pass

    def advance(*steps):
        if not joined:
            return
        for k, number in steps:
            last = line - 1
            for step in range(number, last + 1 if number == 3 else number + 1):
                pump(k, step)
                if k == 0:
                    pump(4, step)
                if k == 0 and step == 2:
                    begin_line(2)
                if k == 0 and step == last:
                    begin_across(2)
                if k == 1 and step == last:
                    begin_across(3)
                if k == 2 and step == 1:
                    begin_line(3)
                if step == 1 and k in AROUND:
                    turn(k)

    sel_column = jnp.broadcast_to(sel_ref[...].astype(FULL), (8, slots)).T[:, 0:1].astype(jnp.int32)
    spot_ref[...] = sel_column

    def pick(number, which, dead_zero, out_ref):
        block = 2 * size
        rows = pl.ds(pl.multiple_of(number * block, block), block)
        spots = lax.broadcasted_iota(jnp.int32, (block, seq_len), 1)
        hot = (spots == spot_ref[rows, :]).astype(FULL).astype(LOW)
        got = nn(hot, table[which])
        if dead_zero:
            ids = number * block + lax.broadcasted_iota(jnp.int32, (block, 1), 0)
            got = jnp.where(ids < count, got, 0.0)
        out_ref[rows, :] = got.astype(LOW)

    table_copy(0, tok_any).wait()

    @pl.loop(0, 2)
    def _(number):
        pick(number, 0, False, x_ref)

    advance((0, 1))
    table_copy(1, cot_any).wait()

    @pl.loop(0, 2)
    def _(number):
        pick(number, 1, True, dy_ref)

        @pl.when(number == 0)
        def _():
            advance((1, 1))

    advance((0, 2), (1, 2), (0, 3), (1, 3), (2, 1))

    if joined:
        arrive(4)
        arrive(0)
        arrive(1)
        gains[...] = jnp.concatenate([vg[d][:, :share] for d in range(groups)], axis=1)

    first_gain, gain_row, router_row = gains[0:1, :], gains[1:2, :], gains[2:3, :]

    def weight(k):
        return wg[k].reshape(width, wg.shape[-1])

    w_first = weight(0)
    for t in range(4):
        w4[t] = w_first[:, t * local_width : (t + 1) * local_width]
    def first_norm(number):
        x_rows = x_ref[rows_at(number), :].astype(FULL)
        inverse = mean_square_inverse(x_rows)
        return x_rows, x_rows * inverse, inverse

    for number in range(BLOCKS):
        table[0, number * size : (number + 1) * size, :] = (
            first_norm(number)[1] * first_gain
        ).astype(LOW)
    for t in range(3):
        qkv_ref[t] = nn(table[0, :slots, :], w4[t]).astype(LOW)

    def forward_rows(block):
        start, stop = block * size, (block + 1) * size
        own = start + lax.broadcasted_iota(jnp.int32, (size, 1), 0)
        keys = lax.broadcasted_iota(jnp.int32, (size, stop), 1)
        allowed = keys <= jnp.minimum(own, count - 1)

        def forward_head(head, mixed):
            lanes = head_lanes(local_width, head)
            query = qkv_ref[0, start:stop, :] * (lanes * HEAD_DIM ** (-0.5))
            scores = nt(query, qkv_ref[1, :stop, :])
            scores = jnp.where(allowed, scores, MASKED_SCORE)
            terms = jnp.exp(scores - jnp.max(scores, axis=-1, keepdims=True))
            inverse = 1.0 / jnp.sum(terms, axis=-1, keepdims=True)
            probs = (terms * inverse).astype(LOW)
            return mixed + nn(probs, qkv_ref[2, :stop, :] * lanes)

        mixed = jnp.zeros((size, local_width), FULL)
        for head in range(heads):
            mixed = forward_head(head, mixed)
        o_ref[start:stop, :] = mixed.astype(LOW)

    @pl.loop(0, BLOCKS)
    def _(turn_number):
        number = top - turn_number

        @pl.when(turn_number > 0)
        def _():
            heads_sum.cross(number + 1)

        for block in range(BLOCKS):

            @pl.when(number == block)
            def _():
                forward_rows(block)

        heads_sum.put(number, nt(o_ref[rows_at(number), :], w4[3]))

        @pl.when(turn_number == 0)
        def _():
            advance((2, 2), (3, 1))

    heads_sum.cross(0)
    advance((2, 3), (3, 2), (3, 3))

    def summed(number):
        attended = a_total[number].reshape(size, width).astype(FULL)
        x_rows = x_ref[rows_at(number), :].astype(FULL)
        summed_rows = (x_rows + attended).astype(LOW).astype(FULL)
        inverse = mean_square_inverse(summed_rows)
        return summed_rows * inverse, inverse

    def kept(which, number):
        return which // 2, span((which % 2) * slots + number * size)

    def kept_all(which):
        return table[which // 2, (which % 2) * slots : (which % 2 + 1) * slots, :]

    def up_phase(number):
        heads_sum.arrived(number)
        inner = (summed(number)[0] * gain_row).astype(LOW)
        up = nn(inner, weight(1))
        square = up * up
        bent = jnp.tanh(0.7978845608028654 * (up + 0.044715 * square * up))
        half = 0.5 * (1.0 + bent)
        which, spot = kept(0, number)
        table[which, spot, :] = (up * half).astype(LOW)
        which, spot = kept(1, number)
        table[which, spot, :] = inner
        slope = half + 0.5 * up * (1.0 - bent * bent) * (
            0.7978845608028654 * (1.0 + 3.0 * 0.044715 * square)
        )
        slope_ref[rows_at(number), :] = slope.astype(LOW)
        rows = rows_at(number)
        gate = gate_of(x_ref[rows, :].astype(FULL), router_row)
        which, spot = kept(2, number)
        table[which, spot, :] = (gate * dy_ref[rows, :].astype(FULL)).astype(LOW)

    def back_phase(number):
        rows = rows_at(number)
        which, spot = kept(2, number)
        up_low = (nn(table[which, spot, :], weight(2)) * slope_ref[rows, :].astype(FULL)).astype(LOW)
        which, spot = kept(3, number)
        table[which, spot, :] = up_low
        hidden_sum.put(number, nt(table[which, spot, :], weight(1)))

    heads_sum.finish(top)
    if joined:
        arrive(2)

    @pl.loop(0, BLOCKS + 1)
    def _(turn_number):
        number = top - turn_number

        @pl.when(turn_number > 1)
        def _():
            hidden_sum.cross(number + 2)
            branch_sum.cross(number + 2)

        @pl.when(turn_number < BLOCKS)
        def _():
            up_phase(number)

            @pl.when(number > 0)
            def _():
                heads_sum.finish(number - 1)

        if joined:

            @pl.when(turn_number == 1)
            def _():
                arrive(3)

        @pl.when(turn_number == BLOCKS)
        def _():
            keep(2, tn(kept_all(2), kept_all(0)))
            give(2)

        @pl.when(turn_number > 0)
        def _():
            back_phase(number + 1)
            which, spot = kept(0, number + 1)
            branch_sum.put(number + 1, nt(table[which, spot, :], weight(2)))

    hidden_sum.cross(0)
    branch_sum.cross(0)
    keep(1, tn(kept_all(1), kept_all(3)))
    give(1)

    out_acc[...] = jnp.zeros_like(out_acc)
    dkv[...] = jnp.zeros_like(dkv)
    vacc[...] = jnp.zeros_like(vacc)
    hidden_sum.finish(top)

    def backward_rows(block):
        start, stop = block * size, (block + 1) * size
        own = start + lax.broadcasted_iota(jnp.int32, (1, size), 1)
        keys = lax.broadcasted_iota(jnp.int32, (stop, size), 0)
        allowed = keys <= jnp.minimum(own, count - 1)

        def backward_head(head, dq):
            lanes = head_lanes(local_width, head)
            query = qkv_ref[0, start:stop, :] * (lanes * HEAD_DIM ** (-0.5))
            mixed_grad = do_ref[...] * lanes
            scores = nt(qkv_ref[1, :stop, :], query)
            scores = jnp.where(allowed, scores, MASKED_SCORE)
            terms = jnp.exp(scores - jnp.max(scores, axis=0, keepdims=True))
            total = 1.0 / jnp.sum(terms, axis=0, keepdims=True)
            probs = terms * total
            prob_grad = nt(qkv_ref[2, :stop, :], mixed_grad)
            dots = jnp.sum(prob_grad * probs, axis=0, keepdims=True)
            score_grad = (probs * (prob_grad - dots)).astype(LOW)
            dkv[1, :stop, :] += nn(probs.astype(LOW), mixed_grad)
            dkv[0, :stop, :] += nn(score_grad, query)
            return dq + tn(score_grad, qkv_ref[1, :stop, :] * lanes)

        dq = jnp.zeros((size, local_width), FULL)
        dq = lax.fori_loop(0, heads, backward_head, dq)
        dlow[0, start:stop, :] = (dq * HEAD_DIM ** (-0.5)).astype(LOW)

    @pl.loop(0, BLOCKS)
    def _(turn_number):
        number = top - turn_number
        rows = rows_at(number)

        @pl.when(number > 0)
        def _():
            hidden_sum.finish(number - 1)

        hidden_sum.arrived(number)
        normed, inverse = summed(number)
        grad = h_total[number].reshape(size, width).astype(FULL)
        vacc[1:2, :] += jnp.sum(grad * normed, axis=0, keepdims=True)
        scaled = grad * gain_row
        back = inverse * (scaled - normed * jnp.mean(scaled * normed, axis=-1, keepdims=True))
        back_low = back.astype(LOW)
        dz_ref[rows, :] = back_low
        gate = gate_of(x_ref[rows, :].astype(FULL), router_row)
        attn = (gate * dy_ref[rows, :].astype(FULL) + back_low.astype(FULL)).astype(LOW)
        do_ref[...] = nn(attn, w4[3]).astype(LOW)
        out_acc[...] += tn(attn, o_ref[rows, :])

        @pl.when(turn_number > 0)
        def _():
            input_sum.cross(number + 1)

        for block in range(BLOCKS):

            @pl.when(number == block)
            def _():
                backward_rows(block)

        dlow[1, rows, :] = dkv[0, rows, :].astype(LOW)
        dlow[2, rows, :] = dkv[1, rows, :].astype(LOW)
        part_sum = nt(dlow[0, rows, :], w4[0])
        part_sum += nt(dlow[1, rows, :], w4[1])
        part_sum += nt(dlow[2, rows, :], w4[2])
        heads_sum.drain(number)
        input_sum.put(number, part_sum)
        if joined:
            for when, k, which in ((0, 2, (1, 2)), (1, 2, range(3, line + 1)), (2, 1, (1, 2)), (3, 1, (3,))):

                @pl.when(turn_number == when)
                def _():
                    relay(k, *which)

    input_sum.cross(0)

    @pl.loop(0, BLOCKS)
    def _(number):
        which, spot = kept(0, number)
        table[which, spot, :] = (first_norm(number)[1] * first_gain).astype(LOW)

    blocks = [tn(kept_all(0), dlow[t]) for t in range(3)]
    blocks.append(out_acc[...])
    keep(0, jnp.concatenate(blocks, axis=1))
    give(0)

    branch_sum.finish(top)
    input_sum.finish(top)

    @pl.loop(0, BLOCKS)
    def _(turn_number):
        number = top - turn_number
        rows = rows_at(number)

        @pl.when(number > 0)
        def _():
            branch_sum.finish(number - 1)
            input_sum.finish(number - 1)

        if joined:
            for when, k, which in ((1, 1, range(4, line + 1)), (2, 0, (1, 2)), (3, 0, range(3, line + 1))):

                @pl.when(turn_number == when)
                def _():
                    relay(k, *which)

        branch_sum.arrived(number)
        x_rows, normed, inverse = first_norm(number)
        dy_rows = dy_ref[rows, :].astype(FULL)
        added = a_total[number].reshape(size, width).astype(FULL)
        added = added + m_total[number].reshape(size, width).astype(FULL)
        gate = gate_of(x_rows, router_row)
        gate_grad = jnp.sum(dy_rows * added, axis=-1, keepdims=True)
        logit_grad = gate_grad * gate * (1.0 - gate) * width ** (-0.5)
        branch_sum.drain(number)
        m_total[number] = (x_rows + gate * added).astype(LOW).reshape(2, size // 2, width)
        input_sum.arrived(number)
        grad = d_total[number].reshape(size, width).astype(FULL)
        vacc[0:1, :] += jnp.sum(grad * normed, axis=0, keepdims=True)
        vacc[2:3, :] += jnp.sum(logit_grad * x_rows, axis=0, keepdims=True)
        scaled = grad * first_gain
        back = inverse * (scaled - normed * jnp.mean(scaled * normed, axis=-1, keepdims=True))
        dx_rows = dy_rows + dz_ref[rows, :].astype(FULL) + back + logit_grad * router_row
        input_sum.drain(number)
        d_total[number] = dx_rows.astype(LOW).reshape(2, size // 2, width)

    if joined:
        for d in range(groups):
            vpad[d, :, :share] = vacc[:, d * share : (d + 1) * share]
        for j in range(1, groups):
            to_all(j).start()
        for k in (2, 1, 0):
            collect(k)
        total = vpad[me]
        for j in range(1, groups):
            to_all(j).wait_recv()
            total = total + vr[j - 1]
        vsum_ref[...] = total
        for k in range(5):
            drain_weights(k)
        for k in range(3):
            for j in range(1, line + 1):
                to_pair(k, j).wait_send()
            for j in range(1, line):
                to_line(k, j).wait_send()
        for j in range(1, groups):
            to_all(j).wait_send()
    else:
        vsum_ref[...] = vacc[...]

    @pl.loop(0, BLOCKS)
    def _(number):
        hidden_sum.drain(number)


def adam_update(master, first_moment, second_moment, gradient, step_rate, decay_rate):
    first_new = MOMENT_DECAY * first_moment + (1.0 - MOMENT_DECAY) * gradient
    second_new = SQUARE_DECAY * second_moment + (1.0 - SQUARE_DECAY) * gradient * gradient
    first_hat = first_new / (1.0 - MOMENT_DECAY**STEP)
    second_hat = second_new / (1.0 - SQUARE_DECAY**STEP)
    master_new = master - step_rate * (
        first_hat / (jnp.sqrt(second_hat) + ADAM_EPS) + decay_rate * master
    )
    return (master_new, first_new, second_new)


def last_kernel(cap_ref, sel_ref, vsum_ref, *refs):
    vec_old, (tok, cot, y, dx, gsum), olds, refs = refs[:3], refs[3:8], refs[8:20], refs[20:]
    vec_new, (out, grad), news, refs = refs[:3], refs[3:5], refs[5:17], refs[17:]
    (tok_b, cot_b, y_b, dx_b, gsum_b), olds_b, (out_b, grad_b), news_b = (
        refs[:5],
        refs[5:17],
        refs[17:19],
        refs[19:31],
    )
    row_sems, in_sems, out_sems, done_sems = refs[31:]
    slots, width = y_b.shape
    seq_len = tok_b.shape[0]
    rows = min(SPOT_ROWS, seq_len)
    chunks = seq_len // rows

    small = [pltpu.make_async_copy(gsum, gsum_b, in_sems.at[0])]
    small += [
        pltpu.make_async_copy(old, old_b, in_sems.at[3 + i])
        for i, (old, old_b) in enumerate(zip(olds, olds_b))
    ]
    placed = [
        pltpu.make_async_copy(y, y_b, in_sems.at[1]),
        pltpu.make_async_copy(dx, dx_b, in_sems.at[2]),
    ]
    finished = [
        pltpu.make_async_copy(new_b, new, done_sems.at[i])
        for i, (new, new_b) in enumerate(zip(news, news_b))
    ]

    def part(number):
        return pl.ds(pl.multiple_of(number * rows, rows), rows)

    def load(which, number):
        source, target = ((tok, tok_b), (cot, cot_b))[which]
        return pltpu.make_async_copy(
            source.at[part(number)], target.at[part(number)], row_sems.at[which, number]
        )

    def store(which, number):
        source, target = ((out_b, out), (grad_b, grad))[which]
        return pltpu.make_async_copy(
            source.at[part(number)], target.at[part(number)], out_sems.at[which, number]
        )

    for copy in small[:1] + small[1:] + placed:
        copy.start()

    @pl.loop(0, chunks)
    def _(number):
        load(0, number).start()
        load(1, number).start()

    for copy in small:
        copy.wait()
    local_width = olds_b[0].shape[-1]
    share = vec_old[0].shape[1]
    first = gsum_b[0]
    parts = [first[:, t * local_width : (t + 1) * local_width] for t in range(4)]
    for t in range(3):
        old = [olds_b[4 * i][t] for i in range(3)]
        for i, value in enumerate(adam_update(*old, parts[t], RATE_MATRIX, WEIGHT_DECAY)):
            news_b[4 * i][t] = value
    for number, gradient in ((1, parts[3].T), (2, gsum_b[1]), (3, gsum_b[2])):
        old = [olds_b[number + 4 * i][...] for i in range(3)]
        for i, value in enumerate(adam_update(*old, gradient, RATE_MATRIX, WEIGHT_DECAY)):
            news_b[number + 4 * i][...] = value
    for copy in finished:
        copy.start()
    values = adam_update(*[ref[...] for ref in vec_old], vsum_ref[0:3, :share], RATE_VECTOR, 0.0)
    for ref, value in zip(vec_new, values):
        ref[...] = value

    for copy in placed:
        copy.wait()
    ids = lax.broadcasted_iota(jnp.int32, (1, slots), 1)
    chosen = jnp.where(ids < cap_ref[lax.axis_index("dp")], sel_ref[...], -1)

    @pl.loop(0, chunks)
    def _(number):
        load(0, number).wait()
        load(1, number).wait()
        spots = number * rows + lax.broadcasted_iota(jnp.int32, (rows, slots), 0)
        hot = (spots == chosen).astype(FULL)
        hit = jnp.max(hot, axis=-1, keepdims=True) > 0.5
        hot = hot.astype(LOW)
        kept_rows = tok_b[part(number), :].astype(FULL)
        out_b[part(number), :] = jnp.where(hit, nn(hot, y_b[...]), kept_rows).astype(LOW)
        store(0, number).start()
        kept_rows = cot_b[part(number), :].astype(FULL)
        grad_b[part(number), :] = jnp.where(hit, nn(hot, dx_b[...]), kept_rows)
        store(1, number).start()

    for copy in finished:
        copy.wait()

    @pl.loop(0, chunks)
    def _(number):
        store(0, number).wait()
        store(1, number).wait()


def shape(dims, kind):
    return jax.ShapeDtypeStruct(dims, kind)


IN_VMEM = pl.BlockSpec(memory_space=pltpu.VMEM)
IN_SMEM = pl.BlockSpec(memory_space=pltpu.SMEM)
IN_ANY = pl.BlockSpec(memory_space=pl.ANY)
DMA = pltpu.SemaphoreType.DMA


def params(number=None):
    if number is None:
        return pltpu.CompilerParams(vmem_limit_bytes=VMEM_BYTES)
    return pltpu.CompilerParams(
        vmem_limit_bytes=VMEM_BYTES, collective_id=number, has_side_effects=True
    )


def local(
    tokens,
    cotangent,
    capacity,
    selected,
    qkv_master,
    out_master,
    up_master,
    down_master,
    vec_master,
    qkv_first,
    out_first,
    up_first,
    down_first,
    vec_first,
    qkv_second,
    out_second,
    up_second,
    down_second,
    vec_second,
):
    groups = lax.axis_size("dp")
    me = lax.axis_index("dp")
    share, local_width = qkv_master.shape[1:]
    hidden = up_master.shape[1]
    width = tokens.shape[2]
    seq_len = tokens.shape[1]
    slots = selected.shape[1]
    joined = share % 32 == 0 and groups % 2 == 0 and groups >= 8
    token_rows, cot_rows = tokens[0], cotangent[0]
    line = groups // 2

    quarter = slots // BLOCKS
    half_block = pltpu.VMEM((BLOCKS, quarter // 2, width), LOW)
    both_halves = pltpu.VMEM((BLOCKS, 2, quarter // 2, width), LOW)
    hops = DMA((2, 3, BLOCKS))
    exchange = [both_halves, half_block, half_block, half_block]
    scratch = [
        pltpu.VMEM((2, seq_len, width), LOW),
        DMA((2,)),
        pltpu.VMEM((slots, width), LOW),
        pltpu.VMEM((slots, width), LOW),
        pltpu.VMEM((3, slots, local_width), LOW),
        pltpu.VMEM((slots, local_width), LOW),
        pltpu.VMEM((4, width, local_width), LOW),
        *exchange,
        both_halves,
        hops,
        hops,
        *exchange,
        both_halves,
        hops,
        *exchange,
        hops,
        pltpu.VMEM((slots, hidden), LOW),
        pltpu.VMEM((slots, width), LOW),
        pltpu.VMEM((width, local_width), FULL),
        pltpu.VMEM((2, slots, local_width), FULL),
        pltpu.VMEM((3, slots, local_width), LOW),
        pltpu.VMEM((8, width), FULL),
        pltpu.VMEM((slots, 1), jnp.int32),
        pltpu.VMEM((quarter, local_width), LOW),
    ]
    if joined:
        weights = (qkv_master, out_master, up_master, down_master.T, vec_master)
        scratch += [
            pltpu.VMEM((3, groups, share, width), LOW),
            pltpu.VMEM((8, width), FULL),
            pltpu.VMEM((groups, 8, 128), FULL),
            DMA((5, line - 1)),
            DMA((5, line - 1)),
            DMA((5, line - 1)),
            DMA((5, line - 1)),
            DMA((5, line)),
            DMA((5, line)),
            DMA((5,)),
            DMA((5,)),
            pltpu.VMEM((3, groups, share, width), LOW),
            pltpu.VMEM((3, line, share, width), LOW),
            pltpu.VMEM((3, line, share, width), LOW),
            pltpu.VMEM((3, line - 1, share, width), LOW),
            pltpu.VMEM((groups, 8, 128), FULL),
            pltpu.VMEM((groups - 1, 8, 128), FULL),
            DMA((3, line)),
            DMA((3, line)),
            DMA((3, line - 1)),
            DMA((3, line - 1)),
            DMA((groups - 1,)),
            DMA((groups - 1,)),
        ]
    else:
        first_shard = jnp.concatenate(
            [qkv_master[0], qkv_master[1], qkv_master[2], out_master.T], axis=1
        )
        shard = jnp.stack([first_shard, up_master, down_master.T]).astype(LOW)
        vectors = lax.all_gather(vec_master.astype(LOW), "dp", axis=1, tiled=True)
        weights = (
            lax.all_gather(shard, "dp", axis=1, tiled=True),
            jnp.pad(vectors.astype(FULL), ((0, 5), (0, 0))),
        )
    y_rows, dx_rows, grad_sum, vec_sum = pl.pallas_call(
        functools.partial(main_kernel, groups, joined),
        out_shape=[
            shape((BLOCKS, 2, quarter // 2, width), LOW),
            shape((BLOCKS, 2, quarter // 2, width), LOW),
            shape((3, share if joined else width, width), FULL),
            shape((8, 128 if joined else width), FULL),
        ],
        in_specs=[IN_SMEM, IN_VMEM, IN_ANY, IN_ANY] + [IN_VMEM] * len(weights),
        out_specs=[IN_VMEM] * 4,
        scratch_shapes=scratch,
        compiler_params=params(0),
        name="main",
    )(capacity, selected, token_rows, cot_rows, *weights)
    y_rows, dx_rows = (rows.reshape(slots, width) for rows in (y_rows, dx_rows))

    if not joined:
        grad_sum = lax.psum_scatter(grad_sum, "dp", scatter_dimension=1, tiled=True)
        vec_sum = lax.psum_scatter(vec_sum, "dp", scatter_dimension=1, tiled=True)
    olds = (
        qkv_master, out_master, up_master, down_master.T,
        qkv_first, out_first, up_first, down_first.T,
        qkv_second, out_second, up_second, down_second.T,
    )
    vec_olds = (vec_master, vec_first, vec_second)
    ones = (token_rows, cot_rows, y_rows, dx_rows, grad_sum)
    made = [shape((seq_len, width), LOW), shape((seq_len, width), FULL)]
    made += [shape(old.shape, FULL) for old in olds]
    chunks = seq_len // min(SPOT_ROWS, seq_len)
    *vec_news, block_out, input_grad, q0, o0, u0, d0, q1, o1, u1, d1, q2, o2, u2, d2 = pl.pallas_call(
        last_kernel,
        out_shape=[shape(old.shape, FULL) for old in vec_olds] + made,
        in_specs=[IN_SMEM] + [IN_VMEM] * 5 + [IN_ANY] * 17,
        out_specs=[IN_VMEM] * 3 + [IN_ANY] * 14,
        scratch_shapes=[pltpu.VMEM(array.shape, array.dtype) for array in (*ones, *olds, *made)]
        + [DMA((2, chunks)), DMA((15,)), DMA((2, chunks)), DMA((12,))],
        compiler_params=params(),
        name="last",
    )(capacity, selected, vec_sum, *vec_olds, *ones, *olds)
    v0, v1, v2 = vec_news
    return (
        block_out[None], input_grad[None],
        q0, o0, u0, d0.T, v0, q1, o1, u1, d1.T, v1, q2, o2, u2, d2.T, v2,
    )


def solution(mesh):
    weights = (
        P(None, "dp", "mp"),
        P("mp", "dp"),
        P("dp", "mp"),
        P("mp", "dp"),
        P(None, "dp"),
    )
    rows = (P("dp", None, None), P("dp", None, None))
    return jax.shard_map(
        local,
        mesh=mesh,
        in_specs=(*rows, P(), P("dp", None), *weights * 3),
        out_specs=(*rows, *weights * 3),
        check_vma=False,
    )
```

profile of v0, /device:TPU:0, one launch (start us, length us, event | category | flops | bytes accessed | tf_op | source)
XLA Modules:
  0.0 140.2 jit_solution(10401311513870808929)
XLA Ops:
  0.7 125.2 %main.1 = (bf16[4,2,128,768]{3,2,1,0:T(8,128)(2,1)}, bf16[4,2,128,768]{3,2,1,0:T(8,128)(2,1)}, f32[3,96,768]{2,1,0:T(8,128)}, f32[8,128]{1,0:T(8,128)}) custom-call(s32[8]{0:T(128)} %cap_ref.1, s32[1,1024]{1,0:T(1,128)} %sel_ref.1, bf16[2048,768]{1,0:T(8,128)(2,1)} %bitcast.12, bf16[2048,768]{1,0:T(8,128)(2,1)} %bitcast.14, f32[3,96,192]{2,1,0:T(8,128)} %refs_8_.3, ...), custom_call_target="tpu_custom_call" | custom-call | tf_op jit(solution)/shard_map/main/pallas_call | solution.py:992
  125.8 14.2 %last.1 = (f32[3,96]{1,0:T(4,128)}, f32[3,96]{1,0:T(4,128)}, f32[3,96]{1,0:T(4,128)}, bf16[2048,768]{1,0:T(8,128)(2,1)}, f32[2048,768]{1,0:T(8,128)}, /*index=5*...) custom-call(s32[8]{0:T(128)} %cap_ref.1, ...), custom_call_target="tpu_custom_call" | custom-call | tf_op jit(solution)/shard_map/last/pallas_call | solution.py:1021
where the time goes:
time: 140 us
  Pallas kernels  139 us (99%)
    pallas_call x1, Pallas kernels, local(): pl.pallas_call(functools.partial(main_kernel, groups, joined), out_shape=...  125 us
    pallas_call x1, Pallas kernels, local(): pl.pallas_call(last_kernel, out_shape=[shape(old.shape, FULL) for old in...  14.2 us

commit v1 on v0

--- a/solution.py
+++ b/solution.py
@@ -136,7 +136,8 @@
         masters, refs = refs[:5], refs[5:]
     else:
         (wg, gains), refs = refs[:2], refs[2:]
-    (m_total, d_total, gsum_ref, vsum_ref), refs = refs[:4], refs[4:]
+    (y_any, dx_any, gsum_ref, vsum_ref), refs = refs[:4], refs[4:]
+    (m_total, d_total, row_sems), refs = refs[:3], refs[3:]
     (table, table_sems, x_ref, dy_ref, qkv_ref, o_ref, w4), refs = refs[:7], refs[7:]
     (parts, near, pair, far, a_total, a_sems, d_sems), refs = refs[:7], refs[7:]
     (h_parts, h_near, h_pair, h_far, h_total, h_sems), refs = refs[:6], refs[6:]
@@ -449,8 +450,6 @@
 
     if joined:
         arrive(4)
-        arrive(0)
-        arrive(1)
         gains[...] = jnp.concatenate([vg[d][:, :share] for d in range(groups)], axis=1)
 
     first_gain, gain_row, router_row = gains[0:1, :], gains[1:2, :], gains[2:3, :]
@@ -458,9 +457,6 @@
     def weight(k):
         return wg[k].reshape(width, wg.shape[-1])
 
-    w_first = weight(0)
-    for t in range(4):
-        w4[t] = w_first[:, t * local_width : (t + 1) * local_width]
     def first_norm(number):
         x_rows = x_ref[rows_at(number), :].astype(FULL)
         inverse = mean_square_inverse(x_rows)
@@ -470,6 +466,13 @@
         table[0, number * size : (number + 1) * size, :] = (
             first_norm(number)[1] * first_gain
         ).astype(LOW)
+    if joined:
+        arrive(0)
+        arrive(1)
+        advance((2, 2))
+    w_first = weight(0)
+    for t in range(4):
+        w4[t] = w_first[:, t * local_width : (t + 1) * local_width]
     for t in range(3):
         qkv_ref[t] = nn(table[0, :slots, :], w4[t]).astype(LOW)
 
@@ -502,6 +505,14 @@
         def _():
             heads_sum.cross(number + 1)
 
+        @pl.when(turn_number == 1)
+        def _():
+            advance((3, 1), (2, 3))
+
+        @pl.when(turn_number == 2)
+        def _():
+            advance((3, 2))
+
         for block in range(BLOCKS):
 
             @pl.when(number == block)
@@ -510,12 +521,8 @@
 
         heads_sum.put(number, nt(o_ref[rows_at(number), :], w4[3]))
 
-        @pl.when(turn_number == 0)
-        def _():
-            advance((2, 2), (3, 1))
-
     heads_sum.cross(0)
-    advance((2, 3), (3, 2), (3, 3))
+    advance((3, 3))
 
     def summed(number):
         attended = a_total[number].reshape(size, width).astype(FULL)
@@ -558,6 +565,10 @@
         table[which, spot, :] = up_low
         hidden_sum.put(number, nt(table[which, spot, :], weight(1)))
 
+    def put_branch(number):
+        which, spot = kept(0, number)
+        branch_sum.put(number, nt(table[which, spot, :], weight(2)))
+
     heads_sum.finish(top)
     if joined:
         arrive(2)
@@ -569,7 +580,10 @@
         @pl.when(turn_number > 1)
         def _():
             hidden_sum.cross(number + 2)
-            branch_sum.cross(number + 2)
+
+        @pl.when(turn_number == 2)
+        def _():
+            branch_sum.cross(top)
 
         @pl.when(turn_number < BLOCKS)
         def _():
@@ -593,13 +607,24 @@
         @pl.when(turn_number > 0)
         def _():
             back_phase(number + 1)
-            which, spot = kept(0, number + 1)
-            branch_sum.put(number + 1, nt(table[which, spot, :], weight(2)))
+
+        @pl.when((turn_number > 0) & (turn_number < 3))
+        def _():
+            put_branch(number + 1)
 
     hidden_sum.cross(0)
-    branch_sum.cross(0)
+    branch_sum.cross(top - 1)
     keep(1, tn(kept_all(1), kept_all(3)))
     give(1)
+    for number in range(top - 1):
+        put_branch(top - 2 - number)
+    for number in range(top - 1):
+        branch_sum.cross(top - 2 - number)
+
+    @pl.loop(0, BLOCKS)
+    def _(number):
+        which, spot = kept(0, number)
+        table[which, spot, :] = (first_norm(number)[1] * first_gain).astype(LOW)
 
     out_acc[...] = jnp.zeros_like(out_acc)
     dkv[...] = jnp.zeros_like(dkv)
@@ -680,16 +705,17 @@
 
     input_sum.cross(0)
 
-    @pl.loop(0, BLOCKS)
-    def _(number):
-        which, spot = kept(0, number)
-        table[which, spot, :] = (first_norm(number)[1] * first_gain).astype(LOW)
-
     blocks = [tn(kept_all(0), dlow[t]) for t in range(3)]
     blocks.append(out_acc[...])
     keep(0, jnp.concatenate(blocks, axis=1))
     give(0)
 
+    def rows_out(which, number):
+        held, target = ((m_total, y_any), (d_total, dx_any))[which]
+        return pltpu.make_async_copy(
+            held.at[number], target.at[number], row_sems.at[which, number]
+        )
+
     branch_sum.finish(top)
     input_sum.finish(top)
 
@@ -704,11 +730,18 @@
             input_sum.finish(number - 1)
 
         if joined:
-            for when, k, which in ((1, 1, range(4, line + 1)), (2, 0, (1, 2)), (3, 0, range(3, line + 1))):
+            for when, k, which in (
+                (0, 1, range(4, line + 1)),
+                (1, 0, (1,)),
+                (2, 0, range(2, line)),
+                (3, 0, (line,)),
+            ):
 
                 @pl.when(turn_number == when)
                 def _():
                     relay(k, *which)
+                    if k == 0 and 0 < when < 3:
+                        collect(3 - when)
 
         branch_sum.arrived(number)
         x_rows, normed, inverse = first_norm(number)
@@ -720,6 +753,7 @@
         logit_grad = gate_grad * gate * (1.0 - gate) * width ** (-0.5)
         branch_sum.drain(number)
         m_total[number] = (x_rows + gate * added).astype(LOW).reshape(2, size // 2, width)
+        rows_out(0, number).start()
         input_sum.arrived(number)
         grad = d_total[number].reshape(size, width).astype(FULL)
         vacc[0:1, :] += jnp.sum(grad * normed, axis=0, keepdims=True)
@@ -729,14 +763,14 @@
         dx_rows = dy_rows + dz_ref[rows, :].astype(FULL) + back + logit_grad * router_row
         input_sum.drain(number)
         d_total[number] = dx_rows.astype(LOW).reshape(2, size // 2, width)
+        rows_out(1, number).start()
 
     if joined:
         for d in range(groups):
             vpad[d, :, :share] = vacc[:, d * share : (d + 1) * share]
         for j in range(1, groups):
             to_all(j).start()
-        for k in (2, 1, 0):
-            collect(k)
+        collect(0)
         total = vpad[me]
         for j in range(1, groups):
             to_all(j).wait_recv()
@@ -757,6 +791,8 @@
     @pl.loop(0, BLOCKS)
     def _(number):
         hidden_sum.drain(number)
+        rows_out(0, number).wait()
+        rows_out(1, number).wait()
 
 
 def adam_update(master, first_moment, second_moment, gradient, step_rate, decay_rate):
@@ -927,6 +963,9 @@
     hops = DMA((2, 3, BLOCKS))
     exchange = [both_halves, half_block, half_block, half_block]
     scratch = [
+        both_halves,
+        both_halves,
+        DMA((2, BLOCKS)),
         pltpu.VMEM((2, seq_len, width), LOW),
         DMA((2,)),
         pltpu.VMEM((slots, width), LOW),
@@ -998,7 +1037,7 @@
             shape((8, 128 if joined else width), FULL),
         ],
         in_specs=[IN_SMEM, IN_VMEM, IN_ANY, IN_ANY] + [IN_VMEM] * len(weights),
-        out_specs=[IN_VMEM] * 4,
+        out_specs=[IN_ANY] * 2 + [IN_VMEM] * 2,
         scratch_shapes=scratch,
         compiler_params=params(0),
         name="main",

time: 140 us -> 134 us (0.957)
  Pallas kernels: 139 us -> 133 us
    pallas_call x1, Pallas kernels: 125 us -> 119 us  [local(): pl.pallas_call(functools.partial(main_kernel, groups, joined), out_shape=...]
where the time goes in v1:
time: 134 us
  Pallas kernels  133 us (99%)
    pallas_call x1, Pallas kernels, local(): pl.pallas_call(functools.partial(main_kernel, groups, joined), out_shape=...  119 us
    pallas_call x1, Pallas kernels, local(): pl.pallas_call(last_kernel, out_shape=[shape(old.shape, FULL) for old in...  14.2 us

profile of v1, /device:TPU:0, one launch (start us, length us, event | category | flops | bytes accessed | tf_op | source)
XLA Modules:
  0.0 133.6 jit_solution(8081819217986453643)
XLA Ops:
  0.7 118.6 %main.1 = (bf16[4,2,128,768]{3,2,1,0:T(8,128)(2,1)}, bf16[4,2,128,768]{3,2,1,0:T(8,128)(2,1)}, f32[3,96,768]{2,1,0:T(8,128)}, f32[8,128]{1,0:T(8,128)}) custom-call(s32[8]{0:T(128)} %cap_ref.1, s32[1,1024]{1,0:T(1,128)} %sel_ref.1, bf16[2048,768]{1,0:T(8,128)(2,1)} %bitcast.12, bf16[2048,768]{1,0:T(8,128)(2,1)} %bitcast.14, f32[3,96,192]{2,1,0:T(8,128)} %refs_8_.3, ...), custom_call_target="tpu_custom_call" | custom-call | tf_op jit(solution)/shard_map/main/pallas_call | solution.py:1031
  119.3 14.2 %last.1 = (f32[3,96]{1,0:T(4,128)}, f32[3,96]{1,0:T(4,128)}, f32[3,96]{1,0:T(4,128)}, bf16[2048,768]{1,0:T(8,128)(2,1)}, f32[2048,768]{1,0:T(8,128)}, /*index=5*...) custom-call(s32[8]{0:T(128)} %cap_ref.1, ...), custom_call_target="tpu_custom_call" | custom-call | tf_op jit(solution)/shard_map/last/pallas_call | solution.py:1060

commit v2 on v1

--- a/solution.py
+++ b/solution.py
@@ -850,7 +850,7 @@
             source.at[part(number)], target.at[part(number)], out_sems.at[which, number]
         )
 
-    for copy in small[:1] + small[1:] + placed:
+    for copy in placed:
         copy.start()
 
     @pl.loop(0, chunks)
@@ -858,25 +858,31 @@
         load(0, number).start()
         load(1, number).start()
 
-    for copy in small:
-        copy.wait()
-    local_width = olds_b[0].shape[-1]
-    share = vec_old[0].shape[1]
-    first = gsum_b[0]
-    parts = [first[:, t * local_width : (t + 1) * local_width] for t in range(4)]
-    for t in range(3):
-        old = [olds_b[4 * i][t] for i in range(3)]
-        for i, value in enumerate(adam_update(*old, parts[t], RATE_MATRIX, WEIGHT_DECAY)):
-            news_b[4 * i][t] = value
-    for number, gradient in ((1, parts[3].T), (2, gsum_b[1]), (3, gsum_b[2])):
-        old = [olds_b[number + 4 * i][...] for i in range(3)]
-        for i, value in enumerate(adam_update(*old, gradient, RATE_MATRIX, WEIGHT_DECAY)):
-            news_b[number + 4 * i][...] = value
-    for copy in finished:
-        copy.start()
-    values = adam_update(*[ref[...] for ref in vec_old], vsum_ref[0:3, :share], RATE_VECTOR, 0.0)
-    for ref, value in zip(vec_new, values):
-        ref[...] = value
+        @pl.when(number == 0)
+        def _():
+            for copy in small:
+                copy.start()
+
+    def update():
+        for copy in small:
+            copy.wait()
+        local_width = olds_b[0].shape[-1]
+        share = vec_old[0].shape[1]
+        first = gsum_b[0]
+        parts = [first[:, t * local_width : (t + 1) * local_width] for t in range(4)]
+        for t in range(3):
+            old = [olds_b[4 * i][t] for i in range(3)]
+            for i, value in enumerate(adam_update(*old, parts[t], RATE_MATRIX, WEIGHT_DECAY)):
+                news_b[4 * i][t] = value
+        for number, gradient in ((1, parts[3].T), (2, gsum_b[1]), (3, gsum_b[2])):
+            old = [olds_b[number + 4 * i][...] for i in range(3)]
+            for i, value in enumerate(adam_update(*old, gradient, RATE_MATRIX, WEIGHT_DECAY)):
+                news_b[number + 4 * i][...] = value
+        for copy in finished:
+            copy.start()
+        values = adam_update(*[ref[...] for ref in vec_old], vsum_ref[0:3, :share], RATE_VECTOR, 0.0)
+        for ref, value in zip(vec_new, values):
+            ref[...] = value
 
     for copy in placed:
         copy.wait()
@@ -897,6 +903,10 @@
         kept_rows = cot_b[part(number), :].astype(FULL)
         grad_b[part(number), :] = jnp.where(hit, nn(hot, dx_b[...]), kept_rows)
         store(1, number).start()
+
+        @pl.when(number == 0)
+        def _():
+            update()
 
     for copy in finished:
         copy.wait()

time: 134 us -> 135 us (level)
  no operation moved by 1% of the time
where the time goes in v2:
time: 135 us
  Pallas kernels  134 us (99%)
    pallas_call x1, Pallas kernels, local(): pl.pallas_call(functools.partial(main_kernel, groups, joined), out_shape=...  119 us
    pallas_call x1, Pallas kernels, local(): pl.pallas_call(last_kernel, out_shape=[shape(old.shape, FULL) for old in...  15.2 us

profile of v2, /device:TPU:0, one launch (start us, length us, event | category | flops | bytes accessed | tf_op | source)
XLA Modules:
  0.0 134.7 jit_solution(3351038953501212309)
XLA Ops:
  0.7 118.6 %main.1 = (bf16[4,2,128,768]{3,2,1,0:T(8,128)(2,1)}, bf16[4,2,128,768]{3,2,1,0:T(8,128)(2,1)}, f32[3,96,768]{2,1,0:T(8,128)}, f32[8,128]{1,0:T(8,128)}) custom-call(s32[8]{0:T(128)} %cap_ref.1, s32[1,1024]{1,0:T(1,128)} %sel_ref.1, bf16[2048,768]{1,0:T(8,128)(2,1)} %bitcast.12, bf16[2048,768]{1,0:T(8,128)(2,1)} %bitcast.14, f32[3,96,192]{2,1,0:T(8,128)} %refs_8_.3, ...), custom_call_target="tpu_custom_call" | custom-call | tf_op jit(solution)/shard_map/main/pallas_call | solution.py:1041
  119.3 15.2 %last.1 = (f32[3,96]{1,0:T(4,128)}, f32[3,96]{1,0:T(4,128)}, f32[3,96]{1,0:T(4,128)}, bf16[2048,768]{1,0:T(8,128)(2,1)}, f32[2048,768]{1,0:T(8,128)}, /*index=5*...) custom-call(s32[8]{0:T(128)} %cap_ref.1, ...), custom_call_target="tpu_custom_call" | custom-call | tf_op jit(solution)/shard_map/last/pallas_call | solution.py:1070
